TPU v7x, 32 devices: a whole 2x2x4 slice. The times are simulated.
32 devices in a mesh: clips: 2 (over x), patch: 8 (over z, y), head: 2 (over core).
Axes of the slice: x: 2, y: 2, z: 4, core: 2. Of those that a mesh axis runs over, the one named last changes fastest.
Arguments:
- tokens: bfloat16 [4096, 3072], P(('clips', 'patch', 'head')), parts along dimension 0, may hold values from -6 to 6
- stale_kv: bfloat16 [4096, 2, 1536], P(('clips', 'patch'), None, 'head'), parts along dimension 0, may hold values from -6 to 6
- qkv_weight: bfloat16 [3072, 3, 1536], P(None, None, 'head'), may hold values from -0.109375 to 0.109375
- out_weight: bfloat16 [1536, 3072], P('head'), may hold values from -3 to 3
- modulation: float32 [2, 3, 3072], replicated, may hold values from -2 to 2
Outputs:
- next_tokens: bfloat16 [4096, 3072], P(('clips', 'patch', 'head')), parts along dimension 0
- kv_cache: bfloat16 [4096, 2, 1536], P(('clips', 'patch'), None, 'head'), parts along dimension 0
There are 2 independent parts, one for each index of `clips`. A program takes and returns all parts, laid end to end along the dimension named above; an argument that names none is the same for every part. Nothing has to cross between parts.
All inputs are finite; a program needn't handle non-finite values.
Results may differ from a plain program's by a relative error of at most 0.014.
Values may be sent and summed in bfloat16 or wider, within the bound.
A program may use at most 192 MiB of HBM per device.

v0:
```python
import jax
import jax.numpy as jnp
from jax import lax
from jax.sharding import PartitionSpec as P

HD = 128
STEPS = 2


epsilon = 1e-06


def modulate(state, shift_scale):
    values = state.astype(jnp.float32)
    centre = jnp.mean(values, axis=-1, keepdims=True)
    spread = jnp.mean(jnp.square(values - centre), axis=-1, keepdims=True)
    normed = (values - centre) * lax.rsqrt(spread + epsilon)
    return (normed * (1.0 + shift_scale[0]) + shift_scale[1]).astype(jnp.bfloat16)


def rms_heads(values):
    return values * lax.rsqrt(jnp.mean(jnp.square(values), axis=-1, keepdims=True) + epsilon)


def project(state, weights, shift_scale, head_size):
    hidden = modulate(state, shift_scale)
    row_count = state.shape[0]
    projected = jnp.dot(
        hidden, weights.reshape(weights.shape[0], -1), preferred_element_type=jnp.float32
    )
    separated = projected.reshape(row_count, 3, -1, head_size)
    queries = (rms_heads(separated[:, 0]) * head_size ** (-0.5)).astype(jnp.bfloat16)
    key_heads = rms_heads(separated[:, 1]).astype(jnp.bfloat16).reshape(row_count, -1)
    value_heads = separated[:, 2].astype(jnp.bfloat16).reshape(row_count, -1)
    return (queries, jnp.stack([key_heads, value_heads], axis=1))


def attend(queries, pairs, weight):
    row_count = pairs.shape[0]
    head_count = queries.shape[1]
    head_size = queries.shape[2]
    key_heads = pairs[:, 0].reshape(row_count, head_count, head_size)
    value_heads = pairs[:, 1].reshape(row_count, head_count, head_size)
    scores = jnp.einsum("qhd,khd->qhk", queries, key_heads, preferred_element_type=jnp.float32)
    exponent = jnp.exp(scores) * weight
    probabilities = exponent.astype(jnp.bfloat16)
    numerator = jnp.einsum(
        "qhk,khd->qhd", probabilities, value_heads, preferred_element_type=jnp.float32
    )
    return (numerator, jnp.sum(exponent, axis=-1))


def body(tokens, stale_kv, qkv_weight, out_weight, modulation):
    tok_dev = tokens.shape[0]
    group_rows = tok_dev * lax.axis_size("head")
    own_patch = lax.axis_index("patch")
    token_rows = lax.all_gather(tokens, "head", axis=0, tiled=True)
    own_rows = tokens
    previous = stale_kv
    fresh_pairs = stale_kv
    for step_index in range(STEPS):
        shift_scale = modulation[step_index]
        queries, fresh_pairs = project(token_rows, qkv_weight, shift_scale, HD)
        numerator, denominator = attend(queries, fresh_pairs, 1.0)

        def fold_keys(carried, incoming):
            positions = jnp.arange(incoming.shape[0], dtype=jnp.int32)
            weight = (positions // group_rows != own_patch).astype(jnp.float32)
            addition = attend(queries, incoming, weight)
            return (carried[0] + addition[0], carried[1] + addition[1])

        if step_index == 0:
            numerator, denominator = fold_keys(
                (numerator, denominator), lax.all_gather(previous, "patch", axis=0, tiled=True)
            )
        else:
            numerator, denominator = fold_keys(
                (numerator, denominator), lax.all_gather(previous, "patch", axis=0, tiled=True)
            )
        output = (numerator / denominator[..., None]).astype(jnp.bfloat16).reshape(group_rows, -1)
        gate_scale = 1.0 + shift_scale[2]
        summed = lax.psum_scatter(
            jnp.dot(output, out_weight, preferred_element_type=jnp.float32).astype(jnp.bfloat16),
            "head",
            scatter_dimension=0,
            tiled=True,
        ).astype(jnp.float32)
        own_rows = (own_rows.astype(jnp.float32) + gate_scale * summed).astype(jnp.bfloat16)
        if step_index + 1 < STEPS:
            token_rows = lax.all_gather(own_rows, "head", axis=0, tiled=True)
        previous = fresh_pairs
    return (own_rows, fresh_pairs)


def solution(mesh):
    in_specs = (
        P(("clips", "patch", "head"), None),
        P(("clips", "patch"), None, "head"),
        P(None, None, "head"),
        P("head", None),
        P(),
    )
    out_specs = (P(("clips", "patch", "head"), None), P(("clips", "patch"), None, "head"))
    return jax.shard_map(body, mesh=mesh, in_specs=in_specs, out_specs=out_specs, check_vma=False)
```

profile of v0, /device:TPU:0, one launch (start us, length us, event | category | flops | bytes accessed | tf_op | source)
XLA Modules:
  0.0 308.8 jit_solution(9107390627012133044)
XLA Ops:
  7.2 0.7 all-gather.5.cloned.1.call-update
  7.9 3.0 copy.57
  11.1 18.7 %copy.53 = bf16[3072,3,768]{0,2,1:T(8,128)(2,1)} copy(bf16[3072,3,768]{2,0,1:T(8,128)(2,1)} %param.7) | data formatting | bytes 28311552 | tf_op args[2]
  30.4 1.8 convert_reduce_fusion.1
  32.3 2.1 fusion.12
  34.4 7.8 %fusion.17 = f32[256,3,6,128]{0,3,2,1:T(8,128)S(1)} fusion(bf16[3,6,128,3072]{3,2,1,0:T(8,128)(2,1)} %bitcast.141, bf16[256,3072]{1,0:T(8,128)(2,1)S(1)} %copy-done.7, f32[3072]{0:T(1024)S(1)} %bitcast.157, f32[3072]{0:T(1024)S(1)} %bitcast.158, f32[256]{0:T(256)S(1)} %add_rsqrt_fusion.5, f32[256]{0:T(256)S(1)} %broadcast_multiply_fusion.1), kind=kOutput, calls=%fused_computation.29 | convolution fusion | flops 3628597248 | bytes 18114560 | tf_op jit(solution)/shard_map/dot_general | solution.py:28
  42.4 1.3 copy-done
  43.7 1.3 bitcast_reduce_fusion.3
  45.0 80.9 %all-gather.7.cloned.1.call-done = bf16[2048,2,768]{0,2,1:T(8,128)(2,1)} async-done(((bf16[256,2,768]{0,2,1:T(8,128)(2,1)}), bf16[2048,2,768]{0,2,1:T(8,128)(2,1)}) %all-gather.7.cloned.1.call-update) | async-done | bytes 6291472 | tf_op jit(solution)/shard_map/all_gather | solution.py:74
  125.8 5.5 %fusion.63 = (bf16[2048,1,768]{0,2,1:T(8,128)(2,1)S(1)}, bf16[2048,1,768]{0,2,1:T(8,128)(2,1)}) fusion(bf16[2048,2,768]{0,2,1:T(8,128)(2,1)} %all-gather.7.cloned.1.call-done), kind=kLoop, calls=%fused_computation.111 | loop fusion | bytes 12582912 | tf_op jit(solution)/shard_map/slice | solution.py:42
  131.4 2.4 bitcast_reduce_fusion.1
  133.8 5.0 %fusion.30 = f32[256,6,128]{0,2,1:T(8,128)} fusion(bf16[2048,6,128]{0,2,1:T(8,128)(2,1)} %bitcast.145, f32[6,256,2048]{2,1,0:T(8,128)S(1)} %get-tuple-element.23, f32[2048]{0:T(1024)S(1)} %fusion.54), kind=kOutput, calls=%fused_computation.48 | convolution fusion | flops 811597824 | bytes 16523264 | tf_op jit(solution)/shard_map/qhk,khd->qhd/dot_general | solution.py:47
  138.8 1.9 fusion.36
  140.7 4.9 %convolution_convert_fusion.1 = bf16[256,3072]{1,0:T(8,128)(2,1)} fusion(bf16[256,768]{0,1:T(8,128)(2,1)S(1)} %bitcast.151, bf16[768,3072]{1,0:T(8,128)(2,1)} %param.8), kind=kOutput, calls=%fused_computation.15 | convolution fusion | flops 1208745984 | bytes 6684672 | tf_op jit(solution)/shard_map/dot_general | solution.py:83
  145.7 1.6 copy-done.2
  147.5 0.9 pad_maximum_fusion
  148.6 4.4 %reduce-scatter.3.cloned.1.call-done = bf16[128,3072]{1,0:T(8,128)(2,1)} async-done(((bf16[256,3072]{1,0:T(8,128)(2,1)}), bf16[128,3072]{1,0:T(8,128)(2,1)}) %reduce-scatter.3.cloned.1.call-update) | async-done | bytes 786448 | tf_op jit(solution)/shard_map/reduce_scatter | solution.py:82
  153.0 2.2 add_convert_fusion.1
  155.5 101.3 %all-gather.11.cloned.1.call-done = bf16[2048,2,768]{0,2,1:T(8,128)(2,1)} async-done(((bf16[256,2,768]{0,2,1:T(8,128)(2,1)}), bf16[2048,2,768]{0,2,1:T(8,128)(2,1)}) %all-gather.11.cloned.1.call-update) | async-done | bytes 6291472 | tf_op jit(solution)/shard_map/all_gather | solution.py:78
  256.9 5.4 %fusion.64 = (bf16[2048,1,768]{0,2,1:T(8,128)(2,1)}, bf16[2048,1,768]{0,2,1:T(8,128)(2,1)S(1)}) fusion(bf16[2048,2,768]{0,2,1:T(8,128)(2,1)} %all-gather.11.cloned.1.call-done), kind=kLoop, calls=%fused_computation.112 | loop fusion | bytes 12582912 | tf_op jit(solution)/shard_map/slice | solution.py:42
  262.2 4.7 %all-gather.9.cloned.1.call-done = bf16[256,3072]{1,0:T(8,128)(2,1)} async-done(((bf16[128,3072]{1,0:T(8,128)(2,1)}), bf16[256,3072]{1,0:T(8,128)(2,1)}) %all-gather.9.cloned.1.call-update) | async-done | bytes 1572880 | tf_op jit(solution)/shard_map/all_gather | solution.py:90
  266.9 1.8 convert_reduce_fusion
  268.7 2.0 fusion.8
  270.7 7.6 %fusion.20 = f32[256,3,6,128]{0,3,2,1:T(8,128)S(1)} fusion(bf16[3,6,128,3072]{3,2,1,0:T(8,128)(2,1)} %bitcast.142, bf16[256,3072]{1,0:T(8,128)(2,1)S(1)} %copy-done.8, f32[3072]{0:T(1024)S(1)} %bitcast.155, f32[3072]{0:T(1024)S(1)} %bitcast.156, f32[256]{0:T(256)S(1)} %add_rsqrt_fusion.4, f32[256]{0:T(256)S(1)} %broadcast_multiply_fusion), kind=kOutput, calls=%fused_computation.31 | convolution fusion | flops 3628597248 | bytes 18114560 | tf_op jit(solution)/shard_map/dot_general | solution.py:28
  279.0 2.1 copy-done.3
  281.1 2.9 bitcast_reduce_fusion
  283.9 2.4 fusion.1
  286.7 2.6 convolution_convert_fusion
  289.4 1.6 copy-done.5
  292.0 1.7 copy.69
  293.7 6.0 %reduce-scatter.5.cloned.1.call-done = bf16[128,3072]{1,0:T(8,128)(2,1)} async-done(((bf16[256,3072]{1,0:T(8,128)(2,1)}), bf16[128,3072]{1,0:T(8,128)(2,1)}) %reduce-scatter.5.cloned.1.call-update) | async-done | bytes 786448 | tf_op jit(solution)/shard_map/reduce_scatter | solution.py:82
  299.8 2.3 add_convert_fusion
  (66 shorter events, 3.5 us)
Async XLA Ops:
  7.2 23.3 %all-gather.5.cloned.1.call-start = ((), (), s32[]{:S(2)}) async-start(), calls=%async_computation.2 | async-start | bytes 2359296 | tf_op jit(solution)/shard_map/all_gather | solution.py:57
  7.9 117.9 %all-gather.7.cloned.1.call-start = ((), (), s32[]{:S(2)}) async-start(), calls=%async_computation.3 | async-start | bytes 7077888 | tf_op jit(solution)/shard_map/all_gather | solution.py:74
  11.0 142.0 %reduce-scatter.3.cloned.1.call-start = ((), (), s32[]{:S(2)}) async-start(), calls=%async_computation.4 | async-start | bytes 2359296 | tf_op jit(solution)/shard_map/reduce_scatter | solution.py:82
  11.0 18.7 %copy-start.10 = (f32[2,3,3072]{2,0,1:T(2,128)S(1)}, f32[2,3,3072]{2,0,1:T(2,128)}, u32[]{:S(2)}) copy-start(f32[2,3,3072]{2,0,1:T(2,128)} %param.9) | copy-start | bytes 221188
  30.4 3.9 %copy-start.7 = (bf16[256,3072]{1,0:T(8,128)(2,1)S(1)}, bf16[256,3072]{1,0:T(8,128)(2,1)}, u32[]{:S(2)}) copy-start(bf16[256,3072]{1,0:T(8,128)(2,1)} %all-gather.5.cloned.1.call-done) | copy-start | bytes 4718596
  42.2 1.5 copy-start
  125.8 5.5 %copy-start.1 = (f32[256,3,6,128]{0,3,2,1:T(8,128)S(1)}, f32[256,3,6,128]{0,3,2,1:T(8,128)}, u32[]{:S(2)}) copy-start(f32[256,3,6,128]{0,3,2,1:T(8,128)} %copy-done) | copy-start | bytes 7077892
  145.6 1.7 copy-start.2
  145.6 1.8 slice-start.2
  145.6 111.2 %all-gather.11.cloned.1.call-start = ((), (), s32[]{:S(2)}) async-start(), calls=%async_computation.6 | async-start | bytes 7077888 | tf_op jit(solution)/shard_map/all_gather | solution.py:78
  147.3 5.7 %copy-start.9 = (bf16[128,3072]{1,0:T(8,128)(2,1)S(1)}, bf16[128,3072]{1,0:T(8,128)(2,1)}, u32[]{:S(2)}) copy-start(bf16[128,3072]{1,0:T(8,128)(2,1)} %param.5) | copy-start | bytes 2359300
  148.5 118.4 %all-gather.9.cloned.1.call-start = ((), (), s32[]{:S(2)}) async-start(), calls=%async_computation.5 | async-start | bytes 2359296 | tf_op jit(solution)/shard_map/all_gather | solution.py:90
  155.3 144.5 %reduce-scatter.5.cloned.1.call-start = ((), (), s32[]{:S(2)}) async-start(), calls=%async_computation.7 | async-start | bytes 2359296 | tf_op jit(solution)/shard_map/reduce_scatter | solution.py:82
  266.9 3.8 %copy-start.8 = (bf16[256,3072]{1,0:T(8,128)(2,1)S(1)}, bf16[256,3072]{1,0:T(8,128)(2,1)}, u32[]{:S(2)}) copy-start(bf16[256,3072]{1,0:T(8,128)(2,1)} %all-gather.9.cloned.1.call-done) | copy-start | bytes 4718596
  278.3 8.1 %copy-start.4 = (f32[256,3,6,128]{0,3,2,1:T(8,128)}, f32[256,3,6,128]{0,3,2,1:T(8,128)S(1)}, u32[]{:S(2)}) copy-start(f32[256,3,6,128]{0,3,2,1:T(8,128)S(1)} %fusion.20) | copy-start | bytes 7077892
  278.3 2.7 copy-start.3
  281.1 5.6 %slice-start = ((s8[4718592]{0:T(1024)(128)(4,1)}), s8[4194304]{0:T(1024)(128)(4,1)S(1)}, s32[]{:S(2)}) async-start(s8[4718592]{0:T(1024)(128)(4,1)} %bitcast.138), calls=%async_computation.8 | async-start | bytes 8388608
  283.9 2.8 slice-start.1
  289.3 1.7 copy-start.5
  289.3 2.0 slice-start.3
  291.7 8.1 %copy-start.6 = (bf16[128,3072]{1,0:T(8,128)(2,1)S(1)}, bf16[128,3072]{1,0:T(8,128)(2,1)}, u32[]{:S(2)}) copy-start(bf16[128,3072]{1,0:T(8,128)(2,1)} %add_convert_fusion.1) | copy-start | bytes 2359300
  291.7 8.1 %copy-start.11 = (f32[1,1,3072]{2,0,1:T(1,128)S(1)}, f32[1,1,3072]{2,0,1:T(1,128)}, u32[]{:S(2)}) copy-start(f32[1,1,3072]{2,0,1:T(1,128)} %get-tuple-element.14) | copy-start | bytes 36868
Sparse Core Ops, SparseCore 0:
  9.5 12.4 all-gather.4
  24.7 101.0 all-gather.6
  145.7 7.2 reduce-scatter.2
  155.7 101.1 all-gather.10
  258.9 7.9 all-gather.8
  289.5 10.2 reduce-scatter.4
where the time goes:
time: 310 us; the launch traced here: 309 us
  waiting for transfers between devices  198 us (64%)
  local copies, waits for them, and re-layouts  42 us (14%)
  matrix products  39.5 us (13%)
  other arithmetic  14.4 us (5%)
  between operations  14.4 us (5%)
    all_gather x2, waiting for transfers between devices, body(): lax.all_gather(previous, 'patch', axis=0, tiled=True)  182 us
    unnamed x31, local copies, waits for them, and re-layouts  30.1 us
    dot_general x2, matrix products, project(): jnp.dot(hidden, weights.reshape(weights.shape[0], -1), preferred_element_...  15.4 us
    slice x2, local copies, waits for them, and re-layouts, attend(): key_heads = pairs[:, 0].reshape(row_count, head_count, head_size)  10.9 us
    reduce_scatter x2, waiting for transfers between devices, body(): lax.psum_scatter(jnp.dot(output, out_weight, preferred_element_type=jnp.f...  10.5 us
    dot_general x4, matrix products, attend(): jnp.einsum('qhk,khd->qhd', probabilities, value_heads, preferred_element_...  9.62 us
    dot_general x2, matrix products, body(): jnp.dot(output, out_weight, preferred_element_type=jnp.float32)  7.5 us
    dot_general x4, matrix products, attend(): jnp.einsum('qhd,khd->qhk', queries, key_heads, preferred_element_type=jnp...  7.01 us
  transfers between devices with their start and end apart: 6, of which 5 were waited for; matrix products, arithmetic and copies ran while one was open for 15% of the time, Pallas kernels for 0%

commit v1 on v0

v1 whole, which is shorter than its diff:
```python
import functools

import jax
import jax.numpy as jnp
from jax import lax
from jax.experimental import pallas as pl
from jax.experimental.pallas import tpu as pltpu
from jax.sharding import PartitionSpec as P

HD = 128
STEPS = 2
EPS = 1e-06
MESH = pl.DeviceIdType.MESH
F32, BF16 = jnp.float32, jnp.bfloat16


def kernel(
    lines,
    tokens_ref,
    stale_ref,
    wqkv_hbm,
    wout_hbm,
    mod_ref,
    next_ref,
    cache_hbm,
    wqkv,
    wout,
    kv,
    last_kv,
    hidden,
    q_own,
    q_peer,
    acc,
    num_out,
    num_in,
    den_out,
    den_in,
    attended,
    part_out,
    part_in,
    state,
    load_sem,
    kv_send,
    kv_recv,
    hid_sem,
    q_sem,
    num_sem,
    den_sem,
    part_sem,
):
    patch, head = lax.axis_index("patch"), lax.axis_index("head")
    a, b = patch // 2, patch % 2
    rows = tokens_ref.shape[0]
    heads = q_own.shape[1]
    size = q_own.shape[2]
    left = {"patch": patch - 2, "head": head}
    right = {"patch": patch + 2, "head": head}
    partner = {"patch": a * 2 + (1 - b), "head": head}
    core = {"patch": patch, "head": 1 - head}
    has_left, has_right = a > 0, a < lines - 1

    loads = [
        pltpu.make_async_copy(wqkv_hbm.at[i], wqkv.at[i], load_sem.at[i]) for i in range(3)
    ]
    loads.append(pltpu.make_async_copy(stale_ref, kv.at[0, a], load_sem.at[3]))
    loads.append(pltpu.make_async_copy(wout_hbm, wout, load_sem.at[4]))

    barrier = pltpu.get_barrier_semaphore()
    pl.semaphore_signal(barrier, inc=1, device_id=partner, device_id_type=MESH)
    pl.semaphore_signal(barrier, inc=1, device_id=core, device_id_type=MESH)

    @pl.when(has_left)
    def _():
        pl.semaphore_signal(barrier, inc=1, device_id=left, device_id_type=MESH)

    @pl.when(has_right)
    def _():
        pl.semaphore_signal(barrier, inc=1, device_id=right, device_id_type=MESH)

    between = has_left & has_right

    @pl.when(between)
    def _():
        pl.semaphore_wait(barrier, 4)

    @pl.when(jnp.logical_not(between))
    def _():
        pl.semaphore_wait(barrier, 3 if lines > 1 else 2)

    def kv_copy(step, slot, way):
        src = kv.at[step, slot]
        return pltpu.make_async_remote_copy(
            src_ref=src,
            dst_ref=kv.at[step, slot],
            send_sem=kv_send.at[step, slot, way],
            recv_sem=kv_recv.at[step, slot],
            device_id=(left, right)[way],
            device_id_type=MESH,
        )

    def start_own(step):
        @pl.when(has_left)
        def _():
            kv_copy(step, a, 0).start()

        @pl.when(has_right)
        def _():
            kv_copy(step, a, 1).start()

    def forward(step, k):
        @pl.when(a + k < lines)
        def _():
            kv_copy(step, a + k, 0).wait_recv()

            @pl.when(has_left)
            def _():
                kv_copy(step, a + k, 0).start()

        @pl.when(a - k >= 0)
        def _():
            kv_copy(step, a - k, 1).wait_recv()

            @pl.when(has_right)
            def _():
                kv_copy(step, a - k, 1).start()

    def drain(step):
        for k in range(lines):

            @pl.when((a + k < lines) & has_left)
            def _():
                kv_copy(step, a + k, 0).wait_send()

            @pl.when((a - k >= 0) & has_right)
            def _():
                kv_copy(step, a - k, 1).wait_send()

    def pair_copy(src, dst, sems, step, target):
        return pltpu.make_async_remote_copy(
            src_ref=src,
            dst_ref=dst,
            send_sem=sems.at[step, 0],
            recv_sem=sems.at[step, 1],
            device_id=target,
            device_id_type=MESH,
        )

    own_half = pl.ds(pl.multiple_of(head * rows, rows), rows)
    peer_half = pl.ds(pl.multiple_of((1 - head) * rows, rows), rows)

    def modulate(step, values):
        centre = jnp.mean(values, axis=-1, keepdims=True)
        shifted = values - centre
        spread = jnp.mean(jnp.square(shifted), axis=-1, keepdims=True)
        normed = shifted * lax.rsqrt(spread + EPS)
        scale = 1.0 + mod_ref[step, 0:1, :]
        hidden[step, own_half, :] = (normed * scale + mod_ref[step, 1:2, :]).astype(BF16)

    def rms(values):
        return values * lax.rsqrt(jnp.mean(jnp.square(values), axis=-1, keepdims=True) + EPS)

    def project(step, which, store):
        @pl.loop(0, heads // 2)
        def _(j):
            columns = pl.ds(pl.multiple_of(j * 2 * HD, 2 * HD), 2 * HD)
            out = jnp.dot(
                hidden[step], wqkv[which, :, columns], preferred_element_type=F32
            )
            store(2 * j, out[:, :HD])
            store(2 * j + 1, out[:, HD:])

    def weigh(queries, keys, values):
        scores = lax.dot_general(
            queries, keys, (((1,), (1,)), ((), ())), preferred_element_type=F32
        )
        weights = jnp.exp(scores).astype(BF16)
        extended = jnp.concatenate([values, jnp.ones_like(values)], axis=1)
        return jnp.dot(weights, extended, preferred_element_type=F32)

    def attend(step, slot):
        @pl.loop(0, heads)
        def _(h):
            keys, values = kv[step, slot, 0, h], kv[step, slot, 1, h]
            acc[1, h] += weigh(q_peer[step, h], keys, values)
            acc[0, h] += weigh(q_own[step, h], keys, values)

    def attend_blocks(step, k):
        @pl.when(a + k < lines)
        def _():
            attend(step, a + k)

        @pl.when(a - k >= 0)
        def _():
            attend(step, a - k)

    loads[3].start()
    for i in range(3):
        loads[i].start()
    loads[4].start()
    loads[3].wait()
    start_own(0)

    for step in range(STEPS):
        if step == 0:
            modulate(step, tokens_ref[...].astype(F32))
        hid = pair_copy(
            hidden.at[step, own_half], hidden.at[step, own_half], hid_sem, step, core
        )
        hid.start()
        hid.wait_recv()

        def store_query(h, out):
            q_own[step, h] = (rms(out) * HD ** (-0.5)).astype(BF16)

        def store_key(h, out):
            value = rms(out).astype(BF16)
            if step == 0:
                kv[1, a, 0, h] = value
            else:
                last_kv[0, h] = value

        def store_value(h, out):
            value = out.astype(BF16)
            if step == 0:
                kv[1, a, 1, h] = value
            else:
                last_kv[1, h] = value

        if step == 0:
            loads[0].wait()
        project(step, 0, store_query)
        queries = pair_copy(q_own.at[step], q_peer.at[step], q_sem, step, partner)
        queries.start()
        if step == 0:
            loads[1].wait()
        if step == 1:
            forward(step, 1)
        project(step, 1, store_key)
        if step == 0:
            loads[2].wait()
        project(step, 2, store_value)
        if step == 1:
            cache = pltpu.make_async_copy(last_kv, cache_hbm, load_sem.at[5])
            cache.start()
        forward(step, 1) if step == 0 else None
        queries.wait_recv()

        @pl.loop(0, heads)
        def _(h):
            acc[1, h] = weigh(q_peer[step, h], kv[step, a, 0, h], kv[step, a, 1, h])
            if step == 0:
                keys, values = kv[1, a, 0, h], kv[1, a, 1, h]
            else:
                keys, values = last_kv[0, h], last_kv[1, h]
            acc[0, h] = weigh(q_own[step, h], keys, values)

        for k in range(1, lines):
            if k > 1:
                forward(step, k)
            if step == 0 and k == max(1, lines - 2):
                start_own(1)
            attend_blocks(step, k)

        lane = lax.broadcasted_iota(jnp.int32, (size, HD), 1)
        packed = jnp.zeros((size, HD), F32)
        for h in range(heads):
            num_out[step, h] = acc[1, h, :, :HD].astype(BF16)
            packed = jnp.where(lane == h, acc[1, h, :, HD:], packed)
        den_out[step] = packed
        dens = pair_copy(den_out.at[step], den_in.at[step], den_sem, step, partner)
        nums = pair_copy(num_out.at[step], num_in.at[step], num_sem, step, partner)
        dens.start()
        nums.start()
        if step == 0:
            loads[4].wait()
        dens.wait_recv()
        nums.wait_recv()
        for h in range(heads):
            numerator = acc[0, h, :, :HD] + num_in[step, h].astype(F32)
            denominator = acc[0, h, :, HD:] + den_in[step, :, h : h + 1]
            attended[:, h * HD : (h + 1) * HD] = (numerator / denominator).astype(BF16)

        part_out[step] = jnp.dot(
            attended[peer_half, :], wout[...], preferred_element_type=F32
        ).astype(BF16)
        part = pair_copy(part_out.at[step], part_in.at[step], part_sem, step, core)
        part.start()
        mine = jnp.dot(attended[own_half, :], wout[...], preferred_element_type=F32)
        part.wait_recv()
        branch = mine + part_in[step].astype(F32)
        before = tokens_ref[...] if step == 0 else state[...]
        after = before.astype(F32) + (1.0 + mod_ref[step, 2:3, :]) * branch
        after = after.astype(BF16)
        if step + 1 < STEPS:
            state[...] = after
            modulate(step + 1, after.astype(F32))
        else:
            next_ref[...] = after
            cache.wait()
        hid.wait_send()
        queries.wait_send()
        dens.wait_send()
        nums.wait_send()
        part.wait_send()
        drain(step)


def body(tokens, stale_kv, qkv_weight, out_weight, modulation):
    rows, width = tokens.shape
    size, _, inner = stale_kv.shape
    heads = inner // HD
    lines = lax.axis_size("patch") // 2
    stale = stale_kv.reshape(size, 2, heads, HD).transpose(1, 2, 0, 3)
    vmem = pl.BlockSpec(memory_space=pltpu.VMEM)
    hbm = pl.BlockSpec(memory_space=pl.ANY)
    dma = pltpu.SemaphoreType.DMA
    next_tokens, cache = pl.pallas_call(
        functools.partial(kernel, lines),
        out_shape=(
            jax.ShapeDtypeStruct((rows, width), BF16),
            jax.ShapeDtypeStruct((2, heads, size, HD), BF16),
        ),
        in_specs=[vmem, hbm, hbm, hbm, vmem],
        out_specs=(vmem, hbm),
        scratch_shapes=[
            pltpu.VMEM((3, width, inner), BF16),
            pltpu.VMEM((inner, width), BF16),
            pltpu.VMEM((STEPS, lines, 2, heads, size, HD), BF16),
            pltpu.VMEM((2, heads, size, HD), BF16),
            pltpu.VMEM((STEPS, size, width), BF16),
            pltpu.VMEM((STEPS, heads, size, HD), BF16),
            pltpu.VMEM((STEPS, heads, size, HD), BF16),
            pltpu.VMEM((2, heads, size, 2 * HD), F32),
            pltpu.VMEM((STEPS, heads, size, HD), BF16),
            pltpu.VMEM((STEPS, heads, size, HD), BF16),
            pltpu.VMEM((STEPS, size, HD), F32),
            pltpu.VMEM((STEPS, size, HD), F32),
            pltpu.VMEM((size, inner), BF16),
            pltpu.VMEM((STEPS, rows, width), BF16),
            pltpu.VMEM((STEPS, rows, width), BF16),
            pltpu.VMEM((rows, width), BF16),
            dma((6,)),
            dma((STEPS, lines, 2)),
            dma((STEPS, lines)),
            dma((STEPS, 2)),
            dma((STEPS, 2)),
            dma((STEPS, 2)),
            dma((STEPS, 2)),
            dma((STEPS, 2)),
        ],
        compiler_params=pltpu.CompilerParams(
            collective_id=0, has_side_effects=True, vmem_limit_bytes=58 * 2**20
        ),
    )(tokens, stale, qkv_weight.transpose(1, 0, 2), out_weight, modulation)
    fresh = cache.transpose(2, 0, 1, 3).reshape(size, 2, inner)
    return next_tokens, fresh


def solution(mesh):
    in_specs = (
        P(("clips", "patch", "head"), None),
        P(("clips", "patch"), None, "head"),
        P(None, None, "head"),
        P("head", None),
        P(),
    )
    out_specs = (P(("clips", "patch", "head"), None), P(("clips", "patch"), None, "head"))
    return jax.shard_map(body, mesh=mesh, in_specs=in_specs, out_specs=out_specs, check_vma=False)
```

time: 310 us -> 142 us (0.46)
  waiting for transfers between devices: 198 us -> 0 us
  Pallas kernels: 0 us -> 130 us
  matrix products: 39.5 us -> 0 us
  local copies, waits for them, and re-layouts: 42 us -> 10.2 us
  other arithmetic: 14.4 us -> 0 us
  between operations: 14.4 us -> 0.65 us
    all_gather x4 -> x0, waiting for transfers between devices: 187 us -> none  [the longest x2 182 us: body(): lax.all_gather(previous, 'patch', axis=0, tiled=True)]
    pallas_call x0 -> x1, Pallas kernels: none -> 130 us  [body(): pl.pallas_call(functools.partial(kernel, lines), out_shape=(jax.ShapeDtyp...]
    dot_general x12 -> x0, matrix products: 39.5 us -> none  [the longest x2 15.4 us: project(): jnp.dot(hidden, weights.reshape(weights.shape[0], -1), preferred_element_...]
    unnamed x31 -> x4, local copies, waits for them, and re-layouts: 30.1 us -> 7.65 us
    slice x8 -> x0, local copies, waits for them, and re-layouts: 11.1 us -> none  [the longest x2 10.9 us: attend(): key_heads = pairs[:, 0].reshape(row_count, head_count, head_size)]
    reduce_scatter x2 -> x0, waiting for transfers between devices: 10.5 us -> none  [body(): lax.psum_scatter(jnp.dot(output, out_weight, preferred_element_type=jnp.f...]
    reduce_sum x6 -> x0, other arithmetic: 7.94 us -> none  [the longest x2 4.05 us: modulate(): spread = jnp.mean(jnp.square(values - centre), axis=-1, keepdims=True)]
    convert_element_type x5 -> x0, other arithmetic: 4.7 us -> none  [the longest x2 4.5 us: body(): (own_rows.astype(jnp.float32) + gate_scale * summed).astype(jnp.bfloat16)]
  transfers between devices with their start and end apart: 6 -> 0, of which waited for: 5 -> 0; matrix products, arithmetic and copies ran while one was open for 15% -> 0% of each run, Pallas kernels for 0% -> 0%
where the time goes in v1:
time: 142 us; the launch traced here: 140 us
  Pallas kernels  130 us (92%)
  local copies, waits for them, and re-layouts  10.2 us (7%)
    pallas_call x1, Pallas kernels, body(): pl.pallas_call(functools.partial(kernel, lines), out_shape=(jax.ShapeDtyp...  130 us
    unnamed x4, local copies, waits for them, and re-layouts  7.65 us

profile of v1, /device:TPU:0, one launch (start us, length us, event | category | flops | bytes accessed | tf_op | source)
XLA Modules:
  0.0 140.5 jit_solution(11376826356109112552)
XLA Ops:
  0.6 1.6 %copy.10.mod_ref = f32[2,3,3072]{2,1,0:T(4,128)} copy(f32[2,3,3072]{2,0,1:T(2,128)} %param.9) | data formatting | bytes 147456 | tf_op args[4]
  2.2 2.2 %copy.8 = bf16[256,2,768]{0,2,1:T(8,128)(2,1)S(1)} copy(bf16[256,2,768]{2,1,0:T(2,128)(2,1)} %param.6) | data formatting | bytes 1572864 | tf_op args[1]
  4.4 1.2 copy.9
  5.6 129.6 %shard_map.68 = (bf16[128,3072]{1,0:T(8,128)(2,1)}, bf16[2,6,256,128]{3,2,1,0:T(8,128)(2,1)}) custom-call(bf16[128,3072]{1,0:T(8,128)(2,1)} %tokens_ref.1, bf16[2,6,256,128]{3,2,1,0:T(8,128)(2,1)} %bitcast.6, bf16[3,3072,768]{2,1,0:T(8,128)(2,1)} %bitcast.5, bf16[768,3072]{1,0:T(8,128)(2,1)} %wout_hbm.1, f32[2,3,3072]{2,1,0:T(4,128)} %copy.10.mod_ref), custom_call_target="tpu_custom_call" | custom-call | tf_op jit(solution)/shard_map/pallas_call | solution.py:317
  135.2 1.4 copy.11
  136.6 1.8 %copy.12 = bf16[256,2,768]{2,1,0:T(2,128)(2,1)} copy(bf16[256,2,768]{0,2,1:T(8,128)(2,1)S(1)} %bitcast.7) | data formatting | bytes 1572864
  138.4 2.1 %copy.14 = bf16[128,3072]{1,0:T(8,128)(2,1)} copy(bf16[128,3072]{1,0:T(8,128)(2,1)} %get-tuple-element.10) | data formatting | bytes 1572864

commit v2 on v1

v2 whole, which is shorter than its diff:
```python
import functools

import jax
import jax.numpy as jnp
from jax import lax
from jax.experimental import pallas as pl
from jax.experimental.pallas import tpu as pltpu
from jax.sharding import PartitionSpec as P

HD = 128
STEPS = 2
EPS = 1e-06
MESH = pl.DeviceIdType.MESH
F32, BF16 = jnp.float32, jnp.bfloat16


def kernel(
    lines,
    tokens_ref,
    stale_ref,
    wqkv_hbm,
    wout_hbm,
    mod_ref,
    next_ref,
    cache_hbm,
    wqkv,
    wout,
    kv,
    last_kv,
    hidden,
    q_own,
    q_peer,
    acc,
    q_help,
    help_acc,
    num_out,
    num_in,
    ret_out,
    ret_in,
    attended,
    part_out,
    part_in,
    state,
    load_sem,
    stale_sem,
    cache_sem,
    kv_send,
    kv_recv,
    hid_sem,
    q_sem,
    num_sem,
    help_sem,
    ret_sem,
    part_sem,
):
    patch, head = lax.axis_index("patch"), lax.axis_index("head")
    a, b = patch // 2, patch % 2
    rows = tokens_ref.shape[0]
    heads = q_own.shape[1]
    size = q_own.shape[2]
    half = heads // 2
    aided = lines >= 4
    left = {"patch": patch - 2, "head": head}
    right = {"patch": patch + 2, "head": head}
    partner = {"patch": a * 2 + (1 - b), "head": head}
    core = {"patch": patch, "head": 1 - head}
    has_left, has_right = a > 0, a < lines - 1

    loads = [
        pltpu.make_async_copy(wqkv_hbm.at[i], wqkv.at[i], load_sem.at[i]) for i in range(3)
    ]
    loads.append(pltpu.make_async_copy(wout_hbm, wout, load_sem.at[3]))
    stales = [
        pltpu.make_async_copy(
            stale_ref.at[i, :, h * HD : (h + 1) * HD], kv.at[0, a, i, h], stale_sem.at[i, h]
        )
        for i in range(2)
        for h in range(heads)
    ]
    caches = [
        pltpu.make_async_copy(
            last_kv.at[i, h], cache_hbm.at[i, :, h * HD : (h + 1) * HD], cache_sem.at[i, h]
        )
        for i in range(2)
        for h in range(heads)
    ]

    barrier = pltpu.get_barrier_semaphore()
    pl.semaphore_signal(barrier, inc=1, device_id=partner, device_id_type=MESH)
    pl.semaphore_signal(barrier, inc=1, device_id=core, device_id_type=MESH)

    @pl.when(has_left)
    def _():
        pl.semaphore_signal(barrier, inc=1, device_id=left, device_id_type=MESH)

    @pl.when(has_right)
    def _():
        pl.semaphore_signal(barrier, inc=1, device_id=right, device_id_type=MESH)

    between = has_left & has_right
    is_end = jnp.logical_not(between)
    if aided:
        is_helper = (a == 1) | (a == lines - 2)
        helper = {"patch": patch + 2 - 4 * (a // (lines - 1)), "head": head}
        aided_end = {"patch": patch - 2 + 4 * (a // (lines - 2)), "head": head}
    send_left = [has_left, a > 1 if aided else has_left]
    send_right = [has_right, a < lines - 2 if aided else has_right]

    def takes(group, present):
        return present & between if aided and group == 1 else present

    @pl.when(between)
    def _():
        pl.semaphore_wait(barrier, 4)

    @pl.when(jnp.logical_not(between))
    def _():
        pl.semaphore_wait(barrier, 3 if lines > 1 else 2)

    def kv_copy(step, slot, group, way):
        part = pl.ds(group * half, half)
        return pltpu.make_async_remote_copy(
            src_ref=kv.at[step, slot, :, part],
            dst_ref=kv.at[step, slot, :, part],
            send_sem=kv_send.at[step, slot, group, way],
            recv_sem=kv_recv.at[step, slot, group],
            device_id=(left, right)[way],
            device_id_type=MESH,
        )

    def start_own(step):
        for group in (1, 0):

            @pl.when(send_left[group])
            def _():
                kv_copy(step, a, group, 0).start()

            @pl.when(send_right[group])
            def _():
                kv_copy(step, a, group, 1).start()

    def forward(step, k, group):
        @pl.when(takes(group, a + k < lines))
        def _():
            kv_copy(step, a + k, group, 0).wait_recv()

            @pl.when(send_left[group])
            def _():
                kv_copy(step, a + k, group, 0).start()

        @pl.when(takes(group, a - k >= 0))
        def _():
            kv_copy(step, a - k, group, 1).wait_recv()

            @pl.when(send_right[group])
            def _():
                kv_copy(step, a - k, group, 1).start()

    def drain(step):
        for k in range(lines):
            for group in range(2):

                @pl.when((a + k < lines) & send_left[group])
                def _():
                    kv_copy(step, a + k, group, 0).wait_send()

                @pl.when((a - k >= 0) & send_right[group])
                def _():
                    kv_copy(step, a - k, group, 1).wait_send()

    def pair_copy(src, dst, sems, step, target, which=0):
        return pltpu.make_async_remote_copy(
            src_ref=src,
            dst_ref=dst,
            send_sem=sems.at[step, which, 0],
            recv_sem=sems.at[step, which, 1],
            device_id=target,
            device_id_type=MESH,
        )

    own_half = pl.ds(pl.multiple_of(head * rows, rows), rows)
    peer_half = pl.ds(pl.multiple_of((1 - head) * rows, rows), rows)

    def modulate(step, values):
        centre = jnp.mean(values, axis=-1, keepdims=True)
        shifted = values - centre
        spread = jnp.mean(jnp.square(shifted), axis=-1, keepdims=True)
        normed = shifted * lax.rsqrt(spread + EPS)
        scale = 1.0 + mod_ref[0, step : step + 1, :]
        hidden[step, own_half, :] = (normed * scale + mod_ref[1, step : step + 1, :]).astype(BF16)

    def rms(values):
        return values * lax.rsqrt(jnp.mean(jnp.square(values), axis=-1, keepdims=True) + EPS)

    def project(step, which, store):
        @pl.loop(0, heads // 2)
        def _(j):
            columns = pl.ds(pl.multiple_of(j * 2 * HD, 2 * HD), 2 * HD)
            out = jnp.dot(
                hidden[step], wqkv[which, :, columns], preferred_element_type=F32
            )
            store(2 * j, out[:, :HD])
            store(2 * j + 1, out[:, HD:])

    def weigh(queries, keys, values):
        scores = lax.dot_general(
            queries, keys, (((1,), (1,)), ((), ())), preferred_element_type=F32
        )
        weights = jnp.exp(scores).astype(BF16)
        extended = jnp.concatenate([values, jnp.ones_like(values)], axis=1)
        return jnp.dot(weights, extended, preferred_element_type=F32)

    def attend(step, slot, group):
        @pl.loop(group * half, (group + 1) * half)
        def _(h):
            keys, values = kv[step, slot, 0, h], kv[step, slot, 1, h]
            acc[1, h] += weigh(q_peer[step, h], keys, values)
            acc[0, h] += weigh(q_own[step, h], keys, values)

    def attend_blocks(step, k, group):
        @pl.when(takes(group, a + k < lines))
        def _():
            attend(step, a + k, group)

        @pl.when(takes(group, a - k >= 0))
        def _():
            attend(step, a - k, group)

    def aid(step, slot, first):
        @pl.loop(0, half)
        def _(h):
            keys, values = kv[step, slot, 0, half + h], kv[step, slot, 1, half + h]
            for i in range(2):
                sums = weigh(q_help[step, i, h], keys, values)
                help_acc[i, h] = sums if first else help_acc[i, h] + sums

    def aid_blocks(step, k):
        @pl.when((a == 1) & (a + k < lines))
        def _():
            aid(step, a + k, False)

        @pl.when((a == lines - 2) & (a - k >= 0))
        def _():
            aid(step, a - k, False)

    lane = lax.broadcasted_iota(jnp.int32, (size, HD), 1)

    def pack(totals):
        packed = jnp.zeros((size, HD), F32)
        for j, total in enumerate(totals):
            high = total.astype(BF16).astype(F32)
            packed = jnp.where(lane == j, high, packed)
            packed = jnp.where(lane == len(totals) + j, total - high, packed)
        return packed.astype(BF16)

    def unpack(packed, j, count):
        high = packed[:, j : j + 1].astype(F32)
        return high + packed[:, count + j : count + j + 1].astype(F32)

    for copy in stales:
        copy.start()
    for copy in loads:
        copy.start()
    for copy in stales:
        copy.wait()
    start_own(0)

    for step in range(STEPS):
        if step == 0:
            modulate(step, tokens_ref[...].astype(F32))
        hid = pair_copy(
            hidden.at[step, own_half], hidden.at[step, own_half], hid_sem, step, core
        )
        hid.start()
        hid.wait_recv()

        def store_query(h, out):
            q_own[step, h] = (rms(out) * HD ** (-0.5)).astype(BF16)

        def store_key(h, out):
            value = rms(out).astype(BF16)
            if step == 0:
                kv[1, a, 0, h] = value
            else:
                last_kv[0, h] = value

        def store_value(h, out):
            value = out.astype(BF16)
            if step == 0:
                kv[1, a, 1, h] = value
            else:
                last_kv[1, h] = value

        if step == 0:
            loads[0].wait()
        project(step, 0, store_query)
        queries = [
            pair_copy(
                q_own.at[step, pl.ds(g * half, half)],
                q_peer.at[step, pl.ds(g * half, half)],
                q_sem,
                step,
                partner,
                g,
            )
            for g in range(2)
        ]
        queries[1].start()
        queries[0].start()
        if aided:
            asks = [
                pair_copy(
                    source.at[step, pl.ds(half, half)],
                    q_help.at[step, i],
                    help_sem,
                    step,
                    helper,
                    i,
                )
                for i, source in enumerate((q_own, q_peer))
            ]
            answer = pair_copy(ret_out.at[step], ret_in.at[step], ret_sem, step, aided_end)

            @pl.when(is_end)
            def _():
                asks[0].start()

        if step == 0:
            loads[1].wait()
        if step == 1:
            forward(step, 1, 1)
            forward(step, 1, 0)
        project(step, 1, store_key)
        if step == 0:
            loads[2].wait()
        project(step, 2, store_value)
        if step == 1:
            for copy in caches:
                copy.start()
        queries[1].wait_recv()
        if aided:

            @pl.when(is_end)
            def _():
                asks[1].start()

        if step == 0:
            forward(step, 1, 1)
            forward(step, 1, 0)
        queries[0].wait_recv()

        @pl.loop(0, heads)
        def _(h):
            acc[1, h] = weigh(q_peer[step, h], kv[step, a, 0, h], kv[step, a, 1, h])
            if step == 0:
                keys, values = kv[1, a, 0, h], kv[1, a, 1, h]
            else:
                keys, values = last_kv[0, h], last_kv[1, h]
            acc[0, h] = weigh(q_own[step, h], keys, values)

        if aided:

            @pl.when(is_helper)
            def _():
                asks[0].wait_recv()
                asks[1].wait_recv()
                aid(step, a, True)

        nums = [
            pair_copy(num_out.at[step, g], num_in.at[step, g], num_sem, step, partner, g)
            for g in range(2)
        ]

        def send_sums(group):
            for h in range(half):
                num_out[step, group, h] = acc[1, group * half + h, :, :HD].astype(BF16)
            num_out[step, group, half] = pack(
                [acc[1, group * half + h, :, HD:] for h in range(half)]
            )
            nums[group].start()

        for k in range(1, lines):
            for group in (1, 0):
                if k > 1:
                    forward(step, k, group)
                attend_blocks(step, k, group)
                if aided and group == 1:
                    aid_blocks(step, k)
                    if k == lines - 2:

                        @pl.when(is_helper)
                        def _():
                            for i in range(2):
                                for h in range(half):
                                    ret_out[step, i * half + h] = help_acc[
                                        i, h, :, :HD
                                    ].astype(BF16)
                            ret_out[step, heads] = pack(
                                [help_acc[i, h, :, HD:] for i in range(2) for h in range(half)]
                            )
                            answer.start()

                if group == 1 and k == lines - 1:
                    if aided:

                        @pl.when(between)
                        def _():
                            send_sums(1)

                    else:
                        send_sums(1)
            if step == 0 and k == max(1, lines - 2):
                start_own(1)
        send_sums(0)
        if aided:

            @pl.when(is_end)
            def _():
                answer.wait_recv()
                for i in range(2):
                    for h in range(half):
                        j = i * half + h
                        acc[i, half + h, :, :HD] += ret_in[step, j].astype(F32)
                        acc[i, half + h, :, HD:] += unpack(ret_in[step, heads], j, heads)
                send_sums(1)

        if step == 0:
            loads[3].wait()
        for group in range(2):
            nums[group].wait_recv()
            for j in range(half):
                h = group * half + j
                numerator = acc[0, h, :, :HD] + num_in[step, group, j].astype(F32)
                denominator = acc[0, h, :, HD:] + unpack(num_in[step, group, half], j, half)
                attended[:, h * HD : (h + 1) * HD] = (numerator / denominator).astype(BF16)

        part_out[step] = jnp.dot(
            attended[peer_half, :], wout[...], preferred_element_type=F32
        ).astype(BF16)
        part = pair_copy(part_out.at[step], part_in.at[step], part_sem, step, core)
        part.start()
        mine = jnp.dot(attended[own_half, :], wout[...], preferred_element_type=F32)
        part.wait_recv()
        branch = mine + part_in[step].astype(F32)
        before = tokens_ref[...] if step == 0 else state[...]
        after = before.astype(F32) + (1.0 + mod_ref[2, step : step + 1, :]) * branch
        after = after.astype(BF16)
        if step + 1 < STEPS:
            state[...] = after
            modulate(step + 1, after.astype(F32))
        else:
            next_ref[...] = after
            for copy in caches:
                copy.wait()
        hid.wait_send()
        part.wait_send()
        for group in range(2):
            queries[group].wait_send()
            nums[group].wait_send()
        if aided:

            @pl.when(is_end)
            def _():
                asks[0].wait_send()
                asks[1].wait_send()

            @pl.when(is_helper)
            def _():
                answer.wait_send()

        drain(step)


def body(tokens, stale_kv, qkv_weight, out_weight, modulation):
    rows, width = tokens.shape
    size, _, inner = stale_kv.shape
    heads = inner // HD
    lines = lax.axis_size("patch") // 2
    stale = stale_kv.transpose(1, 0, 2)
    vmem = pl.BlockSpec(memory_space=pltpu.VMEM)
    hbm = pl.BlockSpec(memory_space=pl.ANY)
    dma = pltpu.SemaphoreType.DMA
    next_tokens, cache = pl.pallas_call(
        functools.partial(kernel, lines),
        out_shape=(
            jax.ShapeDtypeStruct((rows, width), BF16),
            jax.ShapeDtypeStruct((2, size, inner), BF16),
        ),
        in_specs=[vmem, hbm, hbm, hbm, vmem],
        out_specs=(vmem, hbm),
        scratch_shapes=[
            pltpu.VMEM((3, width, inner), BF16),
            pltpu.VMEM((inner, width), BF16),
            pltpu.VMEM((STEPS, lines, 2, heads, size, HD), BF16),
            pltpu.VMEM((2, heads, size, HD), BF16),
            pltpu.VMEM((STEPS, size, width), BF16),
            pltpu.VMEM((STEPS, heads, size, HD), BF16),
            pltpu.VMEM((STEPS, heads, size, HD), BF16),
            pltpu.VMEM((2, heads, size, 2 * HD), F32),
            pltpu.VMEM((STEPS, 2, heads // 2, size, HD), BF16),
            pltpu.VMEM((2, heads // 2, size, 2 * HD), F32),
            pltpu.VMEM((STEPS, 2, heads // 2 + 1, size, HD), BF16),
            pltpu.VMEM((STEPS, 2, heads // 2 + 1, size, HD), BF16),
            pltpu.VMEM((STEPS, heads + 1, size, HD), BF16),
            pltpu.VMEM((STEPS, heads + 1, size, HD), BF16),
            pltpu.VMEM((size, inner), BF16),
            pltpu.VMEM((STEPS, rows, width), BF16),
            pltpu.VMEM((STEPS, rows, width), BF16),
            pltpu.VMEM((rows, width), BF16),
            dma((4,)),
            dma((2, heads)),
            dma((2, heads)),
            dma((STEPS, lines, 2, 2)),
            dma((STEPS, lines, 2)),
            dma((STEPS, 1, 2)),
            dma((STEPS, 2, 2)),
            dma((STEPS, 2, 2)),
            dma((STEPS, 2, 2)),
            dma((STEPS, 1, 2)),
            dma((STEPS, 1, 2)),
        ],
        compiler_params=pltpu.CompilerParams(
            collective_id=0, has_side_effects=True, vmem_limit_bytes=58 * 2**20
        ),
    )(tokens, stale, qkv_weight.transpose(1, 0, 2), out_weight, modulation.transpose(1, 0, 2))
    return next_tokens, cache.transpose(1, 0, 2)


def solution(mesh):
    in_specs = (
        P(("clips", "patch", "head"), None),
        P(("clips", "patch"), None, "head"),
        P(None, None, "head"),
        P("head", None),
        P(),
    )
    out_specs = (P(("clips", "patch", "head"), None), P(("clips", "patch"), None, "head"))
    return jax.shard_map(body, mesh=mesh, in_specs=in_specs, out_specs=out_specs, check_vma=False)
```

time: 142 us -> 147 us (1.035)
  Pallas kernels: 130 us -> 138 us
  local copies, waits for them, and re-layouts: 10.2 us -> 6.98 us
    pallas_call x1, Pallas kernels: 130 us -> 138 us  [body(): pl.pallas_call(functools.partial(kernel, lines), out_shape=(jax.ShapeDtyp...]
    unnamed x4 -> x3, local copies, waits for them, and re-layouts: 7.65 us -> 6.98 us
where the time goes in v2:
time: 147 us; the launch traced here: 146 us
  Pallas kernels  138 us (94%)
  local copies, waits for them, and re-layouts  6.98 us (5%)
    pallas_call x1, Pallas kernels, body(): pl.pallas_call(functools.partial(kernel, lines), out_shape=(jax.ShapeDtyp...  138 us
    unnamed x3, local copies, waits for them, and re-layouts  6.98 us

profile of v2, /device:TPU:0, one launch (start us, length us, event | category | flops | bytes accessed | tf_op | source)
XLA Modules:
  0.0 145.8 jit_solution(15255822226315795434)
XLA Ops:
  0.6 2.1 %copy.10 = bf16[256,2,768]{2,0,1:T(8,128)(2,1)} copy(bf16[256,2,768]{2,1,0:T(2,128)(2,1)} %param.6) | data formatting | bytes 1572864 | tf_op args[1]
  2.7 138.2 %shard_map.68 = (bf16[128,3072]{1,0:T(8,128)(2,1)}, bf16[2,256,768]{2,1,0:T(8,128)(2,1)}) custom-call(bf16[128,3072]{1,0:T(8,128)(2,1)} %tokens_ref.1, bf16[2,256,768]{2,1,0:T(8,128)(2,1)} %bitcast.7, bf16[3,3072,768]{2,1,0:T(8,128)(2,1)} %bitcast.6, bf16[768,3072]{1,0:T(8,128)(2,1)} %wout_hbm.1, f32[3,2,3072]{2,1,0:T(2,128)} %bitcast.9), custom_call_target="tpu_custom_call" | custom-call | tf_op jit(solution)/shard_map/pallas_call | solution.py:483
  140.9 2.8 %copy.8 = bf16[256,2,768]{2,1,0:T(2,128)(2,1)} copy(bf16[256,2,768]{2,0,1:T(8,128)(2,1)} %bitcast.8) | data formatting | bytes 1572864
  143.8 2.1 %copy.12 = bf16[128,3072]{1,0:T(8,128)(2,1)} copy(bf16[128,3072]{1,0:T(8,128)(2,1)} %get-tuple-element.10) | data formatting | bytes 1572864

commit v3 on v2

--- a/solution.py
+++ b/solution.py
@@ -59,7 +59,7 @@
     heads = q_own.shape[1]
     size = q_own.shape[2]
     half = heads // 2
-    aided = lines >= 4
+    aid_steps = [lines >= 4, False]
     left = {"patch": patch - 2, "head": head}
     right = {"patch": patch + 2, "head": head}
     partner = {"patch": a * 2 + (1 - b), "head": head}
@@ -99,15 +99,17 @@
 
     between = has_left & has_right
     is_end = jnp.logical_not(between)
-    if aided:
+    if any(aid_steps):
         is_helper = (a == 1) | (a == lines - 2)
         helper = {"patch": patch + 2 - 4 * (a // (lines - 1)), "head": head}
         aided_end = {"patch": patch - 2 + 4 * (a // (lines - 2)), "head": head}
-    send_left = [has_left, a > 1 if aided else has_left]
-    send_right = [has_right, a < lines - 2 if aided else has_right]
-
-    def takes(group, present):
-        return present & between if aided and group == 1 else present
+    send_left, send_right = [], []
+    for aided in aid_steps:
+        send_left.append([has_left, a > 1 if aided else has_left])
+        send_right.append([has_right, a < lines - 2 if aided else has_right])
+
+    def takes(step, group, present):
+        return present & between if aid_steps[step] and group == 1 else present
 
     @pl.when(between)
     def _():
@@ -128,31 +130,31 @@
             device_id_type=MESH,
         )
 
-    def start_own(step):
+    def start_own(step, leftward, rightward):
         for group in (1, 0):
 
-            @pl.when(send_left[group])
+            @pl.when(send_left[step][group] & leftward)
             def _():
                 kv_copy(step, a, group, 0).start()
 
-            @pl.when(send_right[group])
+            @pl.when(send_right[step][group] & rightward)
             def _():
                 kv_copy(step, a, group, 1).start()
 
     def forward(step, k, group):
-        @pl.when(takes(group, a + k < lines))
+        @pl.when(takes(step, group, a + k < lines))
         def _():
             kv_copy(step, a + k, group, 0).wait_recv()
 
-            @pl.when(send_left[group])
+            @pl.when(send_left[step][group])
             def _():
                 kv_copy(step, a + k, group, 0).start()
 
-        @pl.when(takes(group, a - k >= 0))
+        @pl.when(takes(step, group, a - k >= 0))
         def _():
             kv_copy(step, a - k, group, 1).wait_recv()
 
-            @pl.when(send_right[group])
+            @pl.when(send_right[step][group])
             def _():
                 kv_copy(step, a - k, group, 1).start()
 
@@ -160,11 +162,11 @@
         for k in range(lines):
             for group in range(2):
 
-                @pl.when((a + k < lines) & send_left[group])
+                @pl.when((a + k < lines) & send_left[step][group])
                 def _():
                     kv_copy(step, a + k, group, 0).wait_send()
 
-                @pl.when((a - k >= 0) & send_right[group])
+                @pl.when((a - k >= 0) & send_right[step][group])
                 def _():
                     kv_copy(step, a - k, group, 1).wait_send()
 
@@ -218,11 +220,11 @@
             acc[0, h] += weigh(q_own[step, h], keys, values)
 
     def attend_blocks(step, k, group):
-        @pl.when(takes(group, a + k < lines))
+        @pl.when(takes(step, group, a + k < lines))
         def _():
             attend(step, a + k, group)
 
-        @pl.when(takes(group, a - k >= 0))
+        @pl.when(takes(step, group, a - k >= 0))
         def _():
             attend(step, a - k, group)
 
@@ -263,9 +265,13 @@
         copy.start()
     for copy in stales:
         copy.wait()
-    start_own(0)
+    start_own(0, a >= 0, a >= 0)
+
+    early_left = (a == lines - 1) | (a == 1)
+    early_right = (a == 0) | (a == lines - 2)
 
     for step in range(STEPS):
+        aided = aid_steps[step]
         if step == 0:
             modulate(step, tokens_ref[...].astype(F32))
         hid = pair_copy(
@@ -327,9 +333,6 @@
 
         if step == 0:
             loads[1].wait()
-        if step == 1:
-            forward(step, 1, 1)
-            forward(step, 1, 0)
         project(step, 1, store_key)
         if step == 0:
             loads[2].wait()
@@ -347,6 +350,7 @@
         if step == 0:
             forward(step, 1, 1)
             forward(step, 1, 0)
+            start_own(1, early_left, early_right)
         queries[0].wait_recv()
 
         @pl.loop(0, heads)
@@ -358,14 +362,6 @@
                 keys, values = last_kv[0, h], last_kv[1, h]
             acc[0, h] = weigh(q_own[step, h], keys, values)
 
-        if aided:
-
-            @pl.when(is_helper)
-            def _():
-                asks[0].wait_recv()
-                asks[1].wait_recv()
-                aid(step, a, True)
-
         nums = [
             pair_copy(num_out.at[step, g], num_in.at[step, g], num_sem, step, partner, g)
             for g in range(2)
@@ -384,22 +380,6 @@
                 if k > 1:
                     forward(step, k, group)
                 attend_blocks(step, k, group)
-                if aided and group == 1:
-                    aid_blocks(step, k)
-                    if k == lines - 2:
-
-                        @pl.when(is_helper)
-                        def _():
-                            for i in range(2):
-                                for h in range(half):
-                                    ret_out[step, i * half + h] = help_acc[
-                                        i, h, :, :HD
-                                    ].astype(BF16)
-                            ret_out[step, heads] = pack(
-                                [help_acc[i, h, :, HD:] for i in range(2) for h in range(half)]
-                            )
-                            answer.start()
-
                 if group == 1 and k == lines - 1:
                     if aided:
 
@@ -410,9 +390,24 @@
                     else:
                         send_sums(1)
             if step == 0 and k == max(1, lines - 2):
-                start_own(1)
+                start_own(1, jnp.logical_not(early_left), jnp.logical_not(early_right))
         send_sums(0)
         if aided:
+
+            @pl.when(is_helper)
+            def _():
+                asks[0].wait_recv()
+                asks[1].wait_recv()
+                aid(step, a, True)
+                for k in range(1, lines):
+                    aid_blocks(step, k)
+                for i in range(2):
+                    for h in range(half):
+                        ret_out[step, i * half + h] = help_acc[i, h, :, :HD].astype(BF16)
+                ret_out[step, heads] = pack(
+                    [help_acc[i, h, :, HD:] for i in range(2) for h in range(half)]
+                )
+                answer.start()
 
             @pl.when(is_end)
             def _():
@@ -439,6 +434,9 @@
         ).astype(BF16)
         part = pair_copy(part_out.at[step], part_in.at[step], part_sem, step, core)
         part.start()
+        if step == 0:
+            forward(1, 1, 1)
+            forward(1, 1, 0)
         mine = jnp.dot(attended[own_half, :], wout[...], preferred_element_type=F32)
         part.wait_recv()
         branch = mine + part_in[step].astype(F32)

time: 147 us -> 135 us (0.918)
  Pallas kernels: 138 us -> 127 us
    pallas_call x1, Pallas kernels: 138 us -> 127 us  [body(): pl.pallas_call(functools.partial(kernel, lines), out_shape=(jax.ShapeDtyp...]
where the time goes in v3:
time: 135 us
  Pallas kernels  127 us (94%)
  local copies, waits for them, and re-layouts  6.98 us (5%)
    pallas_call x1, Pallas kernels, body(): pl.pallas_call(functools.partial(kernel, lines), out_shape=(jax.ShapeDtyp...  127 us
    unnamed x3, local copies, waits for them, and re-layouts  6.98 us

profile of v3, /device:TPU:0, one launch (start us, length us, event | category | flops | bytes accessed | tf_op | source)
XLA Modules:
  0.0 135.0 jit_solution(12755278154527030980)
XLA Ops:
  0.6 2.1 %copy.10 = bf16[256,2,768]{2,0,1:T(8,128)(2,1)} copy(bf16[256,2,768]{2,1,0:T(2,128)(2,1)} %param.6) | data formatting | bytes 1572864 | tf_op args[1]
  2.7 127.4 %shard_map.68 = (bf16[128,3072]{1,0:T(8,128)(2,1)}, bf16[2,256,768]{2,1,0:T(8,128)(2,1)}) custom-call(bf16[128,3072]{1,0:T(8,128)(2,1)} %tokens_ref.1, bf16[2,256,768]{2,1,0:T(8,128)(2,1)} %bitcast.7, bf16[3,3072,768]{2,1,0:T(8,128)(2,1)} %bitcast.6, bf16[768,3072]{1,0:T(8,128)(2,1)} %wout_hbm.1, f32[3,2,3072]{2,1,0:T(2,128)} %bitcast.9), custom_call_target="tpu_custom_call" | custom-call | tf_op jit(solution)/shard_map/pallas_call | solution.py:481
  130.1 2.8 %copy.8 = bf16[256,2,768]{2,1,0:T(2,128)(2,1)} copy(bf16[256,2,768]{2,0,1:T(8,128)(2,1)} %bitcast.8) | data formatting | bytes 1572864
  132.9 2.1 %copy.12 = bf16[128,3072]{1,0:T(8,128)(2,1)} copy(bf16[128,3072]{1,0:T(8,128)(2,1)} %get-tuple-element.10) | data formatting | bytes 1572864
